TPU v7x, 32 devices: a whole 2x2x4 slice. The times are simulated.
32 devices in a mesh: phase: 4 (over z), dp: 4 (over x, core), mp: 2 (over y).
Axes of the slice: x: 2, y: 2, z: 4, core: 2. Of those that a mesh axis runs over, the one named last changes fastest.
Arguments:
- enc_states: bfloat16 [4, 4, 256, 4096], P('phase', 'dp'), may hold values from -4 to 4
- queries: bfloat16 [4, 4, 128, 512], P('phase', 'dp', None, 'mp'), may hold values from -0.25 to 0.25
- query_segments: int32 [4, 4, 128], P('phase', 'dp'), may hold values from 0 to 7, as said below
- key_segments: int32 [4, 4, 256], P('phase', 'dp'), may hold values from 0 to 7, as said below
- kv_weight: bfloat16 [4, 4096, 2, 512], P('phase', None, None, 'mp'), may hold values from -0.09375 to 0.09375
- ctx_cotangent: bfloat16 [4, 4, 128, 512], P('phase', 'dp', None, 'mp'), may hold values from -16 to 16
Outputs:
- context: bfloat16 [4, 4, 128, 512], P('phase', 'dp', None, 'mp')
- state_grad: bfloat16 [4, 4, 256, 4096], P('phase', 'dp', 'mp')
- kv_weight_grad: bfloat16 [4, 4096, 2, 512], P('phase', 'dp', None, 'mp')
Inputs may be any that keep to these rules, and one draw needn't show every extreme that they name: Along each row of query_segments and of key_segments the example numbers start at 0, never fall and rise by one at a time, every example holding one token or more; key_segments[s, r] and query_segments[s, r] hold the same number of examples; some row holds 8 examples. `key_segments`: see query_segments.
All inputs are finite; a program needn't handle non-finite values.
Results may differ from a plain program's by a relative error of at most 0.0095.
Values may be sent and summed in bfloat16 or wider, within the bound.
A program may use at most 64 MiB of HBM per device.

v0:
```python
import jax
import jax.numpy as jnp
from jax import lax
from jax.sharding import PartitionSpec as P

HEAD = 64


def passed_along(x, axis, by):
    peers = lax.axis_size(axis)
    return lax.ppermute(x, axis, [(i, (i + by) % peers) for i in range(peers)])


def body(enc_states, queries, query_segments, key_segments, kv_weight, ctx_cotangent):
    halfway = lax.axis_size("phase") // 2
    local_states = enc_states[0, 0]
    states = passed_along(local_states, "phase", halfway)
    inner_width = kv_weight.shape[-1]
    model_width = kv_weight.shape[1]
    heads_here = inner_width // HEAD
    flat_weight = kv_weight[0].reshape(model_width, 2 * inner_width)
    key_value = jnp.dot(states, flat_weight, preferred_element_type=jnp.float32).astype(
        jnp.bfloat16
    )
    key_part = key_value[:, :inner_width].reshape(-1, heads_here, HEAD)
    value_part = key_value[:, inner_width:].reshape(-1, heads_here, HEAD)
    query_heads = queries[0, 0].reshape(-1, heads_here, HEAD)
    scores = jnp.einsum("qhd,khd->hqk", query_heads, key_part, preferred_element_type=jnp.float32)
    same_segment = query_segments[0, 0][:, None] == key_segments[0, 0][None, :]
    exponent = jnp.where(same_segment[None], jnp.exp(scores), 0.0)
    attention = exponent / jnp.sum(exponent, axis=-1, keepdims=True)
    rounded_attention = attention.astype(jnp.bfloat16)
    context = jnp.einsum(
        "hqk,khd->qhd", rounded_attention, value_part, preferred_element_type=jnp.float32
    ).astype(jnp.bfloat16)
    context_grad = ctx_cotangent[0, 0].reshape(-1, heads_here, HEAD)
    attention_grad = jnp.einsum(
        "qhd,khd->hqk", context_grad, value_part, preferred_element_type=jnp.float32
    )
    score_grad = attention * (
        attention_grad - jnp.sum(attention * attention_grad, axis=-1, keepdims=True)
    )
    rounded_score = score_grad.astype(jnp.bfloat16)
    key_grad = jnp.einsum(
        "hqk,qhd->khd", rounded_score, query_heads, preferred_element_type=jnp.float32
    )
    value_grad = jnp.einsum(
        "hqk,qhd->khd", rounded_attention, context_grad, preferred_element_type=jnp.float32
    )
    key_value_grad = jnp.concatenate(
        [key_grad.reshape(-1, inner_width), value_grad.reshape(-1, inner_width)], axis=1
    ).astype(jnp.bfloat16)
    summed = lax.psum_scatter(
        lax.dot_general(
            key_value_grad,
            flat_weight,
            (((1,), (1,)), ((), ())),
            preferred_element_type=jnp.float32,
        ).astype(jnp.bfloat16),
        "mp",
        scatter_dimension=0,
        tiled=True,
    ).astype(jnp.float32)
    state_grad = passed_along(summed.astype(jnp.bfloat16), "phase", halfway)
    summed = lax.psum_scatter(
        lax.dot_general(
            states, key_value_grad, (((0,), (0,)), ((), ())), preferred_element_type=jnp.float32
        ).astype(jnp.bfloat16),
        "dp",
        scatter_dimension=0,
        tiled=True,
    ).astype(jnp.float32)
    weight_grad = (summed / lax.axis_size("dp")).astype(jnp.bfloat16)
    rows_here = weight_grad.shape[0]
    return (
        context.reshape(1, 1, -1, inner_width),
        state_grad[None, None],
        weight_grad.reshape(1, rows_here, 2, inner_width),
    )


def solution(mesh):
    placed = (
        P("phase", "dp", None, None),
        P("phase", "dp", None, "mp"),
        P("phase", "dp", None),
        P("phase", "dp", None),
        P("phase", None, None, "mp"),
        P("phase", "dp", None, "mp"),
    )
    return jax.shard_map(
        body,
        mesh=mesh,
        in_specs=placed,
        out_specs=(
            P("phase", "dp", None, "mp"),
            P("phase", "dp", "mp", None),
            P("phase", "dp", None, "mp"),
        ),
        check_vma=False,
    )
```

profile of v0, /device:TPU:0, one launch (start us, length us, event | category | flops | bytes accessed | tf_op | source)
XLA Modules:
  0.0 205.5 jit_solution(14752297619428149911)
XLA Ops:
  7.2 0.0 reduce-scatter.3.cloned.1.call-start
  7.2 4.1 %collective-permute-start = (bf16[256,4096]{1,0:T(8,128)(2,1)}, bf16[256,4096]{1,0:T(8,128)(2,1)S(1)}, u32[]{:S(2)}, u32[]{:S(2)}) collective-permute-start(bf16[256,4096]{1,0:T(8,128)(2,1)} %bitcast.70), channel_id=1, source_target_pairs={{0,16},{8,24},{16,0},{24,8},{1,17},{9,25},{17,1},{25,9},{2,18},{10... | collective-permute-start | bytes 6291464 | tf_op jit(solution)/shard_map/ppermute | solution.py:11
  11.3 0.9 copy.23
  12.3 0.0 copy-start.1
  12.3 1.0 copy.25
  13.3 0.0 copy-start.2
  13.3 0.0 copy-start.4
  13.3 0.0 copy-start.5
  13.3 3.0 %copy.33 = bf16[512,8,2,256]{3,1,2,0:T(8,128)(2,1)S(1)} copy(bf16[512,8,2,256]{3,2,1,0:T(2,128)(2,1)} %bitcast.51) | data formatting | bytes 8388608
  16.3 0.0 copy-start
  16.3 0.0 copy-done.4
  16.3 0.0 copy-done.5
  16.3 0.1 broadcast_compare_fusion
  16.4 0.0 copy-start.3
  16.4 85.7 %collective-permute-done = bf16[256,4096]{1,0:T(8,128)(2,1)S(1)} collective-permute-done((bf16[256,4096]{1,0:T(8,128)(2,1)}, bf16[256,4096]{1,0:T(8,128)(2,1)S(1)}, u32[]{:S(2)}, u32[]{:S(2)}) %collective-permute-start) | collective-permute-done | bytes 2097184 | tf_op jit(solution)/shard_map/ppermute | solution.py:11
  102.1 1.2 convolution_convert_fusion.2
  103.3 0.0 copy-done
  103.4 0.1 copy.22
  103.5 0.1 copy.21
  103.6 0.0 copy-done.1
  103.6 0.0 copy-done.3
  103.6 0.3 fusion.2
  103.9 0.0 copy-done.2
  103.9 0.3 convolution_convert_fusion.3
  104.2 1.1 convolution_bitcast_fusion
  105.3 1.2 multiply_reduce_fusion
  106.5 1.1 convolution_convert_fusion.4
  107.7 4.8 %convolution_convert_fusion.1 = bf16[256,4096]{1,0:T(8,128)(2,1)} fusion(bf16[4096,512]{1,0:T(8,128)(2,1)} %bitcast.50, bf16[256,256]{0,1:T(8,128)(2,1)S(1)} %bitcast.54, bf16[256,256]{0,1:T(8,128)(2,1)S(1)} %bitcast.56), kind=kOutput, calls=%fused_computation.2 | convolution fusion | flops 1075314688 | bytes 6553600 | tf_op jit(solution)/shard_map/dot_general | solution.py:54
  112.5 0.0 reduce-scatter.3.cloned.1.call-update
  112.5 0.0 reduce-scatter.5.cloned.1.call-start
  112.6 3.2 %fusion = bf16[4096,512]{0,1:T(8,128)(2,1)} fusion(bf16[256,4096]{1,0:T(8,128)(2,1)S(1)} %collective-permute-done, bf16[256,256]{0,1:T(8,128)(2,1)S(1)} %bitcast.55, bf16[256,256]{0,1:T(8,128)(2,1)S(1)} %bitcast.57), kind=kOutput, calls=%fused_computation.1 | convolution fusion | flops 1076363264 | bytes 6553600 | tf_op jit(solution)/shard_map/dot_general | solution.py:66
  115.7 0.0 reduce-scatter.5.cloned.1.call-update
  115.8 29.9 %reduce-scatter.3.cloned.1.call-done = bf16[128,4096]{1,0:T(8,128)(2,1)} async-done(((bf16[256,4096]{1,0:T(8,128)(2,1)}), bf16[128,4096]{1,0:T(8,128)(2,1)}) %reduce-scatter.3.cloned.1.call-update) | async-done | bytes 1048592 | tf_op jit(solution)/shard_map/reduce_scatter | solution.py:53
  145.7 2.4 %collective-permute-start.1 = (bf16[128,4096]{1,0:T(8,128)(2,1)}, bf16[128,4096]{1,0:T(8,128)(2,1)S(1)}, u32[]{:S(2)}, u32[]{:S(2)}) collective-permute-start(bf16[128,4096]{1,0:T(8,128)(2,1)} %reduce-scatter.3.cloned.1.call-done), channel_id=1, source_target_pairs={{0,16},{8,24},{16,0},{24,8},{1,17},{9,25},{17,1},{25,9},{2,18},{10... | collective-permute-start | bytes 3145736 | tf_op jit(solution)/shard_map/ppermute | solution.py:11
  148.1 0.2 convolution_convert_fusion.5
  148.3 0.7 copy.28
  149.1 45.1 %collective-permute-done.1 = bf16[128,4096]{1,0:T(8,128)(2,1)S(1)} collective-permute-done((bf16[128,4096]{1,0:T(8,128)(2,1)}, bf16[128,4096]{1,0:T(8,128)(2,1)S(1)}, u32[]{:S(2)}, u32[]{:S(2)}) %collective-permute-start.1) | collective-permute-done | bytes 1048608 | tf_op jit(solution)/shard_map/ppermute | solution.py:11
  194.2 0.0 reduce-scatter.5.cloned.1.call-done
  194.2 1.4 multiply_convert_fusion
  195.6 2.0 copy.29
  197.7 1.0 copy.35
  (1 shorter events, 0.0 us)
Async XLA Ops:
  7.2 138.5 %reduce-scatter.3.cloned.1.call-start = ((), (), s32[]{:S(2)}) async-start(), calls=%async_computation.2 | async-start | bytes 3145728 | tf_op jit(solution)/shard_map/reduce_scatter | solution.py:53
  7.2 94.9 %collective-permute-start = (bf16[256,4096]{1,0:T(8,128)(2,1)}, bf16[256,4096]{1,0:T(8,128)(2,1)S(1)}, u32[]{:S(2)}, u32[]{:S(2)}) collective-permute-start(bf16[256,4096]{1,0:T(8,128)(2,1)} %bitcast.70), channel_id=1, source_target_pairs={{0,16},{8,24},{16,0},{24,8},{1,17},{9,25},{17,1},{25,9},{2,18},{10... | collective-permute-start | bytes 6291464 | tf_op jit(solution)/shard_map/ppermute | solution.py:11
  12.3 91.3 %copy-start.1 = (bf16[1,1,128,256]{2,3,1,0:T(8,128)(2,1)}, bf16[1,1,128,256]{2,3,1,0:T(8,128)(2,1)S(1)}, u32[]{:S(2)}) copy-start(bf16[1,1,128,256]{2,3,1,0:T(8,128)(2,1)S(1)} %copy.23) | copy-start | bytes 196612
  13.3 90.6 %copy-start.2 = (bf16[1,1,128,256]{2,3,1,0:T(8,128)(2,1)}, bf16[1,1,128,256]{2,3,1,0:T(8,128)(2,1)S(1)}, u32[]{:S(2)}) copy-start(bf16[1,1,128,256]{2,3,1,0:T(8,128)(2,1)S(1)} %copy.25) | copy-start | bytes 196612
  13.3 3.0 %copy-start.4 = (s32[1,1,256]{2,1,0:T(1,128)S(1)}, s32[1,1,256]{2,1,0:T(1,128)}, u32[]{:S(2)}) copy-start(s32[1,1,256]{2,1,0:T(1,128)} %param.9) | copy-start | bytes 3076
  13.3 3.0 %copy-start.5 = (s32[1,1,128]{2,1,0:T(1,128)S(1)}, s32[1,1,128]{2,1,0:T(1,128)}, u32[]{:S(2)}) copy-start(s32[1,1,128]{2,1,0:T(1,128)} %param.8) | copy-start | bytes 1540
  16.3 87.1 %copy-start = (bf16[512,8,2,256]{3,1,2,0:T(8,128)(2,1)}, bf16[512,8,2,256]{3,1,2,0:T(8,128)(2,1)S(1)}, u32[]{:S(2)}) copy-start(bf16[512,8,2,256]{3,1,2,0:T(8,128)(2,1)S(1)} %copy.33) | copy-start | bytes 12582916
  16.4 87.2 %copy-start.3 = (pred[128,256]{0,1:T(8,128)(4,1)}, pred[128,256]{0,1:T(8,128)(4,1)S(1)}, u32[]{:S(2)}) copy-start(pred[128,256]{0,1:T(8,128)(4,1)S(1)} %broadcast_compare_fusion) | copy-start | bytes 98308
  112.5 81.7 %reduce-scatter.5.cloned.1.call-start = ((), (), s32[]{:S(2)}) async-start(), calls=%async_computation.3 | async-start | bytes 5242880 | tf_op jit(solution)/shard_map/reduce_scatter | solution.py:65
  145.7 48.5 %collective-permute-start.1 = (bf16[128,4096]{1,0:T(8,128)(2,1)}, bf16[128,4096]{1,0:T(8,128)(2,1)S(1)}, u32[]{:S(2)}, u32[]{:S(2)}) collective-permute-start(bf16[128,4096]{1,0:T(8,128)(2,1)} %reduce-scatter.3.cloned.1.call-done), channel_id=1, source_target_pairs={{0,16},{8,24},{16,0},{24,8},{1,17},{9,25},{17,1},{25,9},{2,18},{10... | collective-permute-start | bytes 3145736 | tf_op jit(solution)/shard_map/ppermute | solution.py:11
Sparse Core Ops, SparseCore 0:
  112.6 33.0 reduce-scatter.2
  148.4 44.4 reduce-scatter.4
where the time goes:
time: 206 us; the launch traced here: 205 us
  waiting for transfers between devices  161 us (78%)
  between operations  14.2 us (7%)
  matrix products  13.5 us (7%)
  local copies, waits for them, and re-layouts  8.88 us (4%)
  starting transfers between devices  6.58 us (3%)
    ppermute x2, waiting for transfers between devices, passed_along(): return lax.ppermute(x, axis, [(i, (i + by) % peers) for i in range(peers)])  131 us
    reduce_scatter x1, waiting for transfers between devices, body(): lax.psum_scatter(lax.dot_general(key_value_grad, flat_weight, (((1,), (1,...  29.9 us
    unnamed x18, local copies, waits for them, and re-layouts  8.66 us
    ppermute x2, starting transfers between devices, passed_along(): return lax.ppermute(x, axis, [(i, (i + by) % peers) for i in range(peers)])  6.5 us
    dot_general x1, matrix products, body(): lax.dot_general(key_value_grad, flat_weight, (((1,), (1,)), ((), ())), pr...  4.84 us
  transfers between devices with their start and end apart: 4, of which 3 were waited for; matrix products, arithmetic and copies ran while one was open for 4% of the time, Pallas kernels for 0%

commit v1 on v0

v1 whole, which is shorter than its diff:
```python
import functools

import jax
import jax.numpy as jnp
from jax import lax
from jax.experimental import pallas as pl
from jax.experimental.pallas import tpu as pltpu
from jax.sharding import PartitionSpec as P

HEAD = 64
IN_COLS = 128
OUT_COLS = 256
AHEAD = 3
LAG = 2
MESH = pl.DeviceIdType.MESH
NT = (((1,), (1,)), ((), ()))
TN = (((0,), (0,)), ((), ()))


def dot(a, b, dims=(((1,), (0,)), ((), ()))):
    return lax.dot_general(a, b, dims, preferred_element_type=jnp.float32)


def kernel(
    phases,
    rings,
    parts,
    enc,
    queries,
    query_segments,
    key_segments,
    weight,
    cotangent,
    ctx_out,
    state_out,
    weight_out,
    held,
    raw,
    flat,
    acc,
    stacked_q,
    stacked_c,
    mask,
    att,
    grad,
    partial,
    mp_in,
    total,
    wpart,
    pair_in,
    keep,
    x_out,
    x_in,
    raw_sem,
    in_send,
    in_recv,
    fwd_send,
    fwd_recv,
    mp_send,
    mp_recv,
    out_send,
    out_recv,
    pair_send,
    pair_recv,
    x_send,
    x_recv,
):
    keys, model = enc.shape
    tokens, width = queries.shape
    heads = width // HEAD
    chips = rings // 2
    chunks = model // IN_COLS
    share = chunks // parts
    steps = model // OUT_COLS
    block = chunks // rings
    pairs = chunks // 2
    rows = keys // parts
    phase, ring, part = lax.axis_index("phase"), lax.axis_index("dp"), lax.axis_index("mp")
    chip, core = ring // 2, ring % 2
    across = {"phase": (phase + phases // 2) % phases}
    others = [(part + 1 + j) % parts for j in range(parts - 1)]
    buddy = {"dp": chip * 2 + 1 - core}
    far = [((chip + 1 + j) % chips) * 2 + core for j in range(chips - 1)]

    barrier = pltpu.get_barrier_semaphore()
    greeted = [across, buddy] + [{"mp": o} for o in others] + [{"dp": f} for f in far]
    for device in greeted:
        pl.semaphore_signal(barrier, inc=1, device_id=device, device_id_type=MESH)

    load = pltpu.make_async_copy(weight, raw, raw_sem)
    load.start()

    def remote(src, dst, send, recv, device):
        return pltpu.make_async_remote_copy(
            src_ref=src, dst_ref=dst, send_sem=send, recv_sem=recv,
            device_id=device, device_id_type=MESH,
        )

    def cols(i, size):
        return pl.ds(pl.multiple_of(i * size, size), size)

    def incoming(k):
        g = part * share + k
        return remote(
            enc.at[:, cols(g, IN_COLS)], held.at[g], in_send.at[k], in_recv.at[k], across
        )

    def forward(k, j):
        g = part * share + k
        return remote(
            held.at[g], held.at[g], fwd_send.at[j * share + k], fwd_recv.at[g], {"mp": others[j]}
        )

    def forwarded(k, j):
        g = others[j] * share + k
        return remote(
            held.at[g], held.at[g], fwd_send.at[j * share + k], fwd_recv.at[g], {"mp": others[j]}
        )

    def mp_out(n, j):
        return remote(
            partial.at[n, cols(others[j], rows), :], mp_in.at[part, n],
            mp_send.at[j * steps + n], mp_recv.at[part * steps + n], {"mp": others[j]},
        )

    def mp_arrived(n, j):
        return remote(
            mp_in.at[others[j], n], mp_in.at[others[j], n],
            mp_send.at[j * steps + n], mp_recv.at[others[j] * steps + n], {"mp": others[j]},
        )

    def outgoing(n):
        return remote(
            total.at[n], state_out.at[:, cols(n, OUT_COLS)], out_send.at[n], out_recv.at[n], across
        )

    def kept(t, parity):
        owner = (chip + 1 + t // block) % chips
        return (owner * 2 + parity) * block + t % block

    def pair(t):
        return remote(
            wpart.at[kept(t, 1 - core)], pair_in.at[t], pair_send.at[t], pair_recv.at[t], buddy
        )

    def crossing(t, device):
        return remote(x_out.at[t], x_in.at[t], x_send.at[t], x_recv.at[t], device)

    def far_of(t):
        return {"dp": ((chip + 1 + t // block) % chips) * 2 + core}

    pl.semaphore_wait(barrier, len(greeted))
    for k in range(min(AHEAD, share)):
        incoming(k).start()

    head_of = lax.broadcasted_iota(jnp.int32, (tokens, width), 1) // HEAD
    for ref, out in ((queries, stacked_q), (cotangent, stacked_c)):
        values = ref[...].astype(jnp.float32)
        for h in range(heads):
            out[h * tokens : (h + 1) * tokens] = jnp.where(head_of == h, values, 0.0).astype(
                jnp.bfloat16
            )
    of_key = jnp.broadcast_to(key_segments[...].astype(jnp.float32), (tokens, keys)).T
    of_query = jnp.broadcast_to(query_segments[...].astype(jnp.float32), (keys, tokens))
    mask[...] = jnp.where(of_key == of_query, 1.0, 0.0)
    acc[...] = jnp.zeros_like(acc)
    load.wait()

    def relay(g):
        here = cols(g, IN_COLS)
        both = raw[here]
        flat[here, :width] = both[:, 0, :]
        flat[here, width:] = both[:, 1, :]

    def project(g):
        acc[...] += dot(held[g], flat[cols(g, IN_COLS), :])

    def arrive(k, carry):
        relay(part * share + k)
        for o in others:
            relay(o * share + k)
        incoming(k).wait_recv()
        for j in range(parts - 1):
            forward(k, j).start()
        incoming(k).wait_send()

        @pl.when(k + AHEAD < share)
        def _():
            incoming(k + AHEAD).start()

        project(part * share + k)

        @pl.when(k > 0)
        def _():
            for j in range(parts - 1):
                forwarded(k - 1, j).wait_recv()
                project(others[j] * share + k - 1)

        return carry

    lax.fori_loop(0, share, arrive, 0)
    for j in range(parts - 1):
        forwarded(share - 1, j).wait_recv()
        project(others[j] * share + share - 1)

    key_part = acc[:, :width].astype(jnp.bfloat16)
    value_part = acc[:, width:].astype(jnp.bfloat16)
    shown = mask[...] > 0.5
    for h in range(heads):
        here = slice(h * tokens, (h + 1) * tokens)
        exponent = jnp.where(shown, jnp.exp(dot(key_part, stacked_q[here], NT)), 0.0)
        attention = exponent * (1.0 / jnp.sum(exponent, axis=0, keepdims=True))
        attention_grad = dot(value_part, stacked_c[here], NT)
        score_grad = attention * (
            attention_grad - jnp.sum(attention * attention_grad, axis=0, keepdims=True)
        )
        att[0, :, here] = score_grad.astype(jnp.bfloat16)
        att[1, :, here] = attention.astype(jnp.bfloat16)
    grad[:, :width] = dot(att[0], stacked_q[...]).astype(jnp.bfloat16)
    grad[:, width:] = dot(att[1], stacked_c[...]).astype(jnp.bfloat16)

    def weigh(g):
        wpart[g] = dot(held[g], grad[...], TN).astype(jnp.bfloat16)

    def back(n, carry):
        @pl.when(n < steps)
        def _():
            partial[n] = dot(grad[...], flat[cols(n, OUT_COLS), :], NT).astype(jnp.bfloat16)
            for j in range(parts - 1):
                mp_out(n, j).start()

        @pl.when(n < pairs)
        def _():
            weigh(kept(n, 1 - core))
            pair(n).start()

        @pl.when(jnp.logical_and(n >= LAG, n < steps + LAG))
        def _():
            old = n - LAG
            summed = partial[old, cols(part, rows), :].astype(jnp.float32)
            for j in range(parts - 1):
                mp_arrived(old, j).wait_recv()
                summed = summed + mp_in[others[j], old].astype(jnp.float32)
            total[old] = summed.astype(jnp.bfloat16)
            outgoing(old).start()

        @pl.when(n < pairs)
        def _():
            weigh(kept(n, core))

        @pl.when(jnp.logical_and(n >= LAG, n < pairs + LAG))
        def _():
            old = n - LAG
            pair(old).wait_recv()
            summed = wpart[kept(old, core)].astype(jnp.float32) + pair_in[old].astype(jnp.float32)

            @pl.when(old < pairs - block)
            def _():
                x_out[old] = summed.astype(jnp.bfloat16)
                crossing(old, far_of(old)).start()

            @pl.when(old >= pairs - block)
            def _():
                keep[old - (pairs - block)] = summed

        return carry

    lax.fori_loop(0, max(steps, pairs) + LAG, back, 0)

    context = jnp.zeros((tokens, width), jnp.float32)
    for h in range(heads):
        one = dot(att[1, :, h * tokens : (h + 1) * tokens], value_part, TN)
        context = jnp.where(head_of == h, one, context)
    ctx_out[...] = context.astype(jnp.bfloat16)

    def finish(q, carry):
        summed = keep[q]
        for j in range(chips - 1):
            crossing(j * block + q, {"dp": far[j]}).wait_recv()
            summed = summed + x_in[j * block + q].astype(jnp.float32)
        weight_out[cols(q, IN_COLS), :] = (summed * (1.0 / rings)).astype(jnp.bfloat16)
        return carry

    lax.fori_loop(0, block, finish, 0)

    def drain(count, one):
        def step(i, carry):
            one(i)
            return carry

        lax.fori_loop(0, count, step, 0)

    for j in range(parts - 1):
        drain(share, lambda k: forward(k, j).wait_send())
        drain(steps, lambda n: mp_out(n, j).wait_send())
    drain(pairs, lambda t: pair(t).wait_send())
    if chips > 1:
        drain(pairs - block, lambda t: crossing(t, far_of(t)).wait_send())
    drain(steps, lambda n: outgoing(n).wait())


def body(enc_states, queries, query_segments, key_segments, kv_weight, ctx_cotangent):
    phases, rings, parts = (lax.axis_size(a) for a in ("phase", "dp", "mp"))
    keys, model = enc_states.shape[2:]
    tokens, width = queries.shape[2:]
    heads = width // HEAD
    chunks = model // IN_COLS
    share, steps, block, pairs = (
        chunks // parts, model // OUT_COLS, chunks // rings, chunks // 2,
    )
    rows = keys // parts
    crossed = max(pairs - block, 1)
    b16, f32 = jnp.bfloat16, jnp.float32
    vmem = pl.BlockSpec(memory_space=pltpu.VMEM)
    hbm = pl.BlockSpec(memory_space=pl.ANY)
    dma = pltpu.SemaphoreType.DMA
    context, state_grad, weight_grad = pl.pallas_call(
        functools.partial(kernel, phases, rings, parts),
        out_shape=(
            jax.ShapeDtypeStruct((tokens, width), b16),
            jax.ShapeDtypeStruct((rows, model), b16),
            jax.ShapeDtypeStruct((model // rings, 2 * width), b16),
        ),
        in_specs=[hbm, vmem, vmem, vmem, hbm, vmem],
        out_specs=(vmem, hbm, vmem),
        scratch_shapes=[
            pltpu.VMEM((chunks, keys, IN_COLS), b16),
            pltpu.VMEM((model, 2, width), b16),
            pltpu.VMEM((model, 2 * width), b16),
            pltpu.VMEM((keys, 2 * width), f32),
            pltpu.VMEM((heads * tokens, width), b16),
            pltpu.VMEM((heads * tokens, width), b16),
            pltpu.VMEM((keys, tokens), f32),
            pltpu.VMEM((2, keys, heads * tokens), b16),
            pltpu.VMEM((keys, 2 * width), b16),
            pltpu.VMEM((steps, keys, OUT_COLS), b16),
            pltpu.VMEM((parts, steps, rows, OUT_COLS), b16),
            pltpu.VMEM((steps, rows, OUT_COLS), b16),
            pltpu.VMEM((chunks, IN_COLS, 2 * width), b16),
            pltpu.VMEM((pairs, IN_COLS, 2 * width), b16),
            pltpu.VMEM((block, IN_COLS, 2 * width), f32),
            pltpu.VMEM((crossed, IN_COLS, 2 * width), b16),
            pltpu.VMEM((crossed, IN_COLS, 2 * width), b16),
            dma,
            dma((share,)),
            dma((share,)),
            dma(((parts - 1) * share,)),
            dma((chunks,)),
            dma(((parts - 1) * steps,)),
            dma((parts * steps,)),
            dma((steps,)),
            dma((steps,)),
            dma((pairs,)),
            dma((pairs,)),
            dma((crossed,)),
            dma((crossed,)),
        ],
        compiler_params=pltpu.CompilerParams(
            collective_id=0, has_side_effects=True, vmem_limit_bytes=56 * 2**20
        ),
        cost_estimate=pl.CostEstimate(
            flops=12 * keys * model * width, bytes_accessed=9 * 2**20, transcendentals=0
        ),
    )(
        enc_states[0, 0], queries[0, 0], query_segments[0], key_segments[0],
        kv_weight[0], ctx_cotangent[0, 0],
    )
    return (
        context[None, None],
        state_grad[None, None],
        weight_grad.reshape(1, -1, 2, width),
    )


def solution(mesh):
    placed = (
        P("phase", "dp", None, None),
        P("phase", "dp", None, "mp"),
        P("phase", "dp", None),
        P("phase", "dp", None),
        P("phase", None, None, "mp"),
        P("phase", "dp", None, "mp"),
    )
    return jax.shard_map(
        body,
        mesh=mesh,
        in_specs=placed,
        out_specs=(
            P("phase", "dp", None, "mp"),
            P("phase", "dp", "mp", None),
            P("phase", "dp", None, "mp"),
        ),
        check_vma=False,
    )
```

time: 206 us -> 115 us (0.56)
  waiting for transfers between devices: 161 us -> 0 us
  Pallas kernels: 0 us -> 108 us
  between operations: 14.2 us -> 0.64 us
  matrix products: 13.5 us -> 0 us
  starting transfers between devices: 6.58 us -> 0 us
  local copies, waits for them, and re-layouts: 8.88 us -> 5.9 us
    ppermute x2 -> x0, waiting for transfers between devices: 131 us -> none  [passed_along(): return lax.ppermute(x, axis, [(i, (i + by) % peers) for i in range(peers)])]
    pallas_call x0 -> x1, Pallas kernels: none -> 108 us  [body(): pl.pallas_call(functools.partial(kernel, phases, rings, parts), out_shape...]
    reduce_scatter x2 -> x0, waiting for transfers between devices: 29.9 us -> none  [the longest x1 29.9 us: body(): lax.psum_scatter(lax.dot_general(key_value_grad, flat_weight, (((1,), (1,...]
    dot_general x8 -> x0, matrix products: 12.3 us -> none  [the longest x1 4.84 us: body(): lax.dot_general(key_value_grad, flat_weight, (((1,), (1,)), ((), ())), pr...]
    ppermute x2 -> x0, starting transfers between devices: 6.5 us -> none  [passed_along(): return lax.ppermute(x, axis, [(i, (i + by) % peers) for i in range(peers)])]
    unnamed x18 -> x2, local copies, waits for them, and re-layouts: 8.66 us -> 3.76 us
    reshape x0 -> x1, local copies, waits for them, and re-layouts: none -> 2.14 us  [body(): weight_grad.reshape(1, -1, 2, width)]
  transfers between devices with their start and end apart: 4 -> 0, of which waited for: 3 -> 0; matrix products, arithmetic and copies ran while one was open for 4% -> 0% of each run, Pallas kernels for 0% -> 0%
where the time goes in v1:
time: 115 us
  Pallas kernels  108 us (94%)
  local copies, waits for them, and re-layouts  5.9 us (5%)
    pallas_call x1, Pallas kernels, body(): pl.pallas_call(functools.partial(kernel, phases, rings, parts), out_shape...  108 us
    unnamed x2, local copies, waits for them, and re-layouts  3.76 us

profile of v1, /device:TPU:0, one launch (start us, length us, event | category | flops | bytes accessed | tf_op | source)
XLA Modules:
  0.0 114.8 jit_solution(5806860348769053141)
XLA Ops:
  0.6 108.2 %shard_map.85 = (bf16[128,256]{1,0:T(8,128)(2,1)}, bf16[128,4096]{1,0:T(8,128)(2,1)}, bf16[1024,512]{1,0:T(8,128)(2,1)}) custom-call(bf16[256,4096]{1,0:T(8,128)(2,1)} %bitcast.11, bf16[128,256]{1,0:T(8,128)(2,1)} %bitcast.12, s32[1,128]{1,0:T(1,128)} %bitcast.15, s32[1,256]{1,0:T(1,128)} %bitcast.14, bf16[4096,2,256]{2,1,0:T(2,128)(2,1)} %bitcast.10, ...), custom_call_target="tpu_custom_call" | custom-call | flops 3221225472 | bytes 9437184 | tf_op jit(solution)/shard_map/pallas_call | solution.py:317
  108.9 2.1 %reshape.9 = bf16[1,1024,2,256]{3,2,1,0:T(2,128)(2,1)} reshape(bf16[1024,512]{1,0:T(8,128)(2,1)} %get-tuple-element.8) | data formatting | bytes 2097152 | tf_op jit(solution)/shard_map/reshape | solution.py:371
  111.0 1.5 %copy.11 = bf16[1,1,128,256]{3,2,1,0:T(8,128)(2,1)} copy(bf16[1,1,128,256]{3,2,1,0:T(8,128)(2,1)} %bitcast.9) | data formatting | bytes 131072
  112.5 2.3 %copy.12 = bf16[1,1,128,4096]{3,2,1,0:T(8,128)(2,1)} copy(bf16[1,1,128,4096]{3,2,1,0:T(8,128)(2,1)} %bitcast.8) | data formatting | bytes 2097152

commit v2 on v1

--- a/solution.py
+++ b/solution.py
@@ -11,7 +11,10 @@
 IN_COLS = 128
 OUT_COLS = 256
 AHEAD = 3
+EARLY = 9
 LAG = 2
+PAIR_LAG = 1
+PIECES = 2
 MESH = pl.DeviceIdType.MESH
 NT = (((1,), (1,)), ((), ()))
 TN = (((0,), (0,)), ((), ()))
@@ -64,6 +67,11 @@
     pair_recv,
     x_send,
     x_recv,
+    final_ctx,
+    final_weight,
+    ctx_sem,
+    weight_sem,
+    turn,
 ):
     keys, model = enc.shape
     tokens, width = queries.shape
@@ -83,7 +91,10 @@
     far = [((chip + 1 + j) % chips) * 2 + core for j in range(chips - 1)]
 
     barrier = pltpu.get_barrier_semaphore()
-    greeted = [across, buddy] + [{"mp": o} for o in others] + [{"dp": f} for f in far]
+    staggered = phases % 4 == 0
+    odd = phase % 2 == 1
+    beside = {"phase": phase + 1 - 2 * (phase % 2)}
+    greeted = [across, buddy] + ([beside] if staggered else []) + [{"mp": o} for o in others] + [{"dp": f} for f in far]
     for device in greeted:
         pl.semaphore_signal(barrier, inc=1, device_id=device, device_id_type=MESH)
 
@@ -150,8 +161,15 @@
         return {"dp": ((chip + 1 + t // block) % chips) * 2 + core}
 
     pl.semaphore_wait(barrier, len(greeted))
-    for k in range(min(AHEAD, share)):
-        incoming(k).start()
+
+    def begin():
+        for k in range(min(AHEAD, share)):
+            incoming(k).start()
+
+    if staggered:
+        pl.when(jnp.logical_not(odd))(begin)
+    else:
+        begin()
 
     head_of = lax.broadcasted_iota(jnp.int32, (tokens, width), 1) // HEAD
     for ref, out in ((queries, stacked_q), (cotangent, stacked_c)):
@@ -175,10 +193,27 @@
     def project(g):
         acc[...] += dot(held[g], flat[cols(g, IN_COLS), :])
 
+    def relay_all(g, carry):
+        relay(g)
+        return carry
+
+    if staggered:
+
+        @pl.when(odd)
+        def _():
+            lax.fori_loop(0, chunks, relay_all, 0)
+            pl.semaphore_wait(turn, 1)
+            begin()
+
+    eager = odd if staggered else phase >= 0
+
     def arrive(k, carry):
-        relay(part * share + k)
-        for o in others:
-            relay(o * share + k)
+        @pl.when(jnp.logical_not(odd) if staggered else eager)
+        def _():
+            relay(part * share + k)
+            for o in others:
+                relay(o * share + k)
+
         incoming(k).wait_recv()
         for j in range(parts - 1):
             forward(k, j).start()
@@ -188,9 +223,17 @@
         def _():
             incoming(k + AHEAD).start()
 
-        project(part * share + k)
-
-        @pl.when(k > 0)
+        if staggered:
+
+            @pl.when(jnp.logical_and(jnp.logical_not(odd), k == max(share - EARLY, 0)))
+            def _():
+                pl.semaphore_signal(turn, inc=1, device_id=beside, device_id_type=MESH)
+
+        @pl.when(eager)
+        def _():
+            project(part * share + k)
+
+        @pl.when(jnp.logical_and(k > 0, eager))
         def _():
             for j in range(parts - 1):
                 forwarded(k - 1, j).wait_recv()
@@ -199,9 +242,18 @@
         return carry
 
     lax.fori_loop(0, share, arrive, 0)
-    for j in range(parts - 1):
-        forwarded(share - 1, j).wait_recv()
-        project(others[j] * share + share - 1)
+
+    def catch_up(k, carry):
+        @pl.when(jnp.logical_not(eager))
+        def _():
+            project(part * share + k)
+
+        for j in range(parts - 1):
+            forwarded(k, j).wait_recv()
+            project(others[j] * share + k)
+        return carry
+
+    lax.fori_loop(jnp.where(eager, share - 1, 0), share, catch_up, 0)
 
     key_part = acc[:, :width].astype(jnp.bfloat16)
     value_part = acc[:, width:].astype(jnp.bfloat16)
@@ -229,11 +281,6 @@
             for j in range(parts - 1):
                 mp_out(n, j).start()
 
-        @pl.when(n < pairs)
-        def _():
-            weigh(kept(n, 1 - core))
-            pair(n).start()
-
         @pl.when(jnp.logical_and(n >= LAG, n < steps + LAG))
         def _():
             old = n - LAG
@@ -244,13 +291,17 @@
             total[old] = summed.astype(jnp.bfloat16)
             outgoing(old).start()
 
-        @pl.when(n < pairs)
-        def _():
-            weigh(kept(n, core))
-
-        @pl.when(jnp.logical_and(n >= LAG, n < pairs + LAG))
-        def _():
-            old = n - LAG
+        at = n - LAG
+
+        @pl.when(jnp.logical_and(at >= 0, at < pairs))
+        def _():
+            weigh(kept(at, 1 - core))
+            pair(at).start()
+            weigh(kept(at, core))
+
+        @pl.when(jnp.logical_and(at >= PAIR_LAG, at < pairs + PAIR_LAG))
+        def _():
+            old = at - PAIR_LAG
             pair(old).wait_recv()
             summed = wpart[kept(old, core)].astype(jnp.float32) + pair_in[old].astype(jnp.float32)
 
@@ -265,20 +316,28 @@
 
         return carry
 
-    lax.fori_loop(0, max(steps, pairs) + LAG, back, 0)
+    lax.fori_loop(0, max(steps, pairs + PAIR_LAG) + LAG, back, 0)
 
     context = jnp.zeros((tokens, width), jnp.float32)
     for h in range(heads):
         one = dot(att[1, :, h * tokens : (h + 1) * tokens], value_part, TN)
         context = jnp.where(head_of == h, one, context)
-    ctx_out[...] = context.astype(jnp.bfloat16)
+    final_ctx[...] = context.astype(jnp.bfloat16)
+    ctx_copy = pltpu.make_async_copy(final_ctx, ctx_out, ctx_sem)
+    ctx_copy.start()
+
+    def weight_copy(q):
+        here = cols(q, IN_COLS)
+        return pltpu.make_async_copy(final_weight.at[here], weight_out.at[here], weight_sem.at[q])
 
     def finish(q, carry):
         summed = keep[q]
         for j in range(chips - 1):
             crossing(j * block + q, {"dp": far[j]}).wait_recv()
             summed = summed + x_in[j * block + q].astype(jnp.float32)
-        weight_out[cols(q, IN_COLS), :] = (summed * (1.0 / rings)).astype(jnp.bfloat16)
+        mean = (summed * (1.0 / rings)).astype(jnp.bfloat16)
+        final_weight[cols(q, IN_COLS)] = mean.reshape(IN_COLS, 2, width)
+        weight_copy(q).start()
         return carry
 
     lax.fori_loop(0, block, finish, 0)
@@ -296,7 +355,33 @@
     drain(pairs, lambda t: pair(t).wait_send())
     if chips > 1:
         drain(pairs - block, lambda t: crossing(t, far_of(t)).wait_send())
+    ctx_copy.wait()
+    drain(block, lambda q: weight_copy(q).wait())
     drain(steps, lambda n: outgoing(n).wait())
+
+
+def hand_over(ctx, state, weight, ctx_out, state_out, weight_out, ctx_buf, state_buf, weight_buf, sems):
+    moves = []
+    for src, buf, dst in (
+        (ctx, ctx_buf, ctx_out), (state, state_buf, state_out), (weight, weight_buf, weight_out),
+    ):
+        pieces = 1 if src is ctx else PIECES
+        size = src.shape[0] // pieces
+        for p in range(pieces):
+            here, i = pl.ds(p * size, size), len(moves)
+            moves.append(
+                (
+                    pltpu.make_async_copy(src.at[here], buf.at[here], sems.at[0, i]),
+                    pltpu.make_async_copy(buf.at[here], dst.at[here], sems.at[1, i]),
+                )
+            )
+    for load, _ in moves:
+        load.start()
+    for load, store in moves:
+        load.wait()
+        store.start()
+    for _, store in moves:
+        store.wait()
 
 
 def body(enc_states, queries, query_segments, key_segments, kv_weight, ctx_cotangent):
@@ -314,15 +399,15 @@
     vmem = pl.BlockSpec(memory_space=pltpu.VMEM)
     hbm = pl.BlockSpec(memory_space=pl.ANY)
     dma = pltpu.SemaphoreType.DMA
-    context, state_grad, weight_grad = pl.pallas_call(
+    results = pl.pallas_call(
         functools.partial(kernel, phases, rings, parts),
         out_shape=(
             jax.ShapeDtypeStruct((tokens, width), b16),
             jax.ShapeDtypeStruct((rows, model), b16),
-            jax.ShapeDtypeStruct((model // rings, 2 * width), b16),
+            jax.ShapeDtypeStruct((model // rings, 2, width), b16),
         ),
         in_specs=[hbm, vmem, vmem, vmem, hbm, vmem],
-        out_specs=(vmem, hbm, vmem),
+        out_specs=(hbm, hbm, hbm),
         scratch_shapes=[
             pltpu.VMEM((chunks, keys, IN_COLS), b16),
             pltpu.VMEM((model, 2, width), b16),
@@ -354,6 +439,11 @@
             dma((pairs,)),
             dma((crossed,)),
             dma((crossed,)),
+            pltpu.VMEM((tokens, width), b16),
+            pltpu.VMEM((model // rings, 2, width), b16),
+            dma,
+            dma((block,)),
+            pltpu.SemaphoreType.REGULAR,
         ],
         compiler_params=pltpu.CompilerParams(
             collective_id=0, has_side_effects=True, vmem_limit_bytes=56 * 2**20
@@ -365,11 +455,14 @@
         enc_states[0, 0], queries[0, 0], query_segments[0], key_segments[0],
         kv_weight[0], ctx_cotangent[0, 0],
     )
-    return (
-        context[None, None],
-        state_grad[None, None],
-        weight_grad.reshape(1, -1, 2, width),
-    )
+    context, state_grad, weight_grad = pl.pallas_call(
+        hand_over,
+        out_shape=tuple(jax.ShapeDtypeStruct(r.shape, r.dtype) for r in results),
+        in_specs=[hbm] * 3,
+        out_specs=(hbm,) * 3,
+        scratch_shapes=[pltpu.VMEM(r.shape, r.dtype) for r in results] + [dma((2, 2 * PIECES + 1))],
+    )(*results)
+    return context[None, None], state_grad[None, None], weight_grad[None]
 
 
 def solution(mesh):

time: 115 us -> 104 us (0.904)
  local copies, waits for them, and re-layouts: 5.9 us -> 0 us
  Pallas kernels: 108 us -> 103 us
    pallas_call x1, Pallas kernels: 108 us -> 101 us  [body(): pl.pallas_call(functools.partial(kernel, phases, rings, parts), out_shape...]
    unnamed x2 -> x0, local copies, waits for them, and re-layouts: 3.76 us -> none
    pallas_call x0 -> x1, Pallas kernels: none -> 2.48 us  [body(): pl.pallas_call(hand_over, out_shape=tuple((jax.ShapeDtypeStruct(r.shape,...]
    reshape x1 -> x0, local copies, waits for them, and re-layouts: 2.14 us -> none  [body(): weight_grad.reshape(1, -1, 2, width)]
where the time goes in v2:
time: 104 us
  Pallas kernels  103 us (99%)
    pallas_call x1, Pallas kernels, body(): pl.pallas_call(functools.partial(kernel, phases, rings, parts), out_shape...  101 us
    pallas_call x1, Pallas kernels, body(): pl.pallas_call(hand_over, out_shape=tuple((jax.ShapeDtypeStruct(r.shape,...  2.48 us

profile of v2, /device:TPU:0, one launch (start us, length us, event | category | flops | bytes accessed | tf_op | source)
XLA Modules:
  0.0 103.8 jit_solution(16198638421674999262)
XLA Ops:
  0.6 100.7 %shard_map.85 = (bf16[128,256]{1,0:T(8,128)(2,1)}, bf16[128,4096]{1,0:T(8,128)(2,1)}, bf16[1024,2,256]{2,1,0:T(2,128)(2,1)}) custom-call(bf16[256,4096]{1,0:T(8,128)(2,1)} %bitcast.10, bf16[128,256]{1,0:T(8,128)(2,1)} %bitcast.13, s32[1,128]{1,0:T(1,128)} %bitcast.17, s32[1,256]{1,0:T(1,128)} %bitcast.16, bf16[4096,2,256]{2,1,0:T(2,128)(2,1)} %bitcast.9, ...), custom_call_target="tpu_custom_call" | custom-call | flops 3221225472 | bytes 9437184 | tf_op jit(solution)/shard_map/pallas_call | solution.py:402
  101.3 2.5 %shard_map.86 = (bf16[128,256]{1,0:T(8,128)(2,1)}, bf16[128,4096]{1,0:T(8,128)(2,1)}, bf16[1024,2,256]{2,1,0:T(2,128)(2,1)}) custom-call(bf16[128,256]{1,0:T(8,128)(2,1)} %get-tuple-element.9.ctx, bf16[128,4096]{1,0:T(8,128)(2,1)} %get-tuple-element.10.state, bf16[1024,2,256]{2,1,0:T(2,128)(2,1)} %get-tuple-element.11.weight), custom_call_target="tpu_custom_call" | custom-call | tf_op jit(solution)/shard_map/pallas_call | solution.py:458

commit v3 on v2

--- a/solution.py
+++ b/solution.py
@@ -11,9 +11,10 @@
 IN_COLS = 128
 OUT_COLS = 256
 AHEAD = 3
-EARLY = 9
+EARLY = 11
 LAG = 2
 PAIR_LAG = 1
+WAIT = 2
 PIECES = 2
 MESH = pl.DeviceIdType.MESH
 NT = (((1,), (1,)), ((), ()))
@@ -77,7 +78,8 @@
     tokens, width = queries.shape
     heads = width // HEAD
     chips = rings // 2
-    chunks = model // IN_COLS
+    in_cols = min(IN_COLS, model // rings)
+    chunks = model // in_cols
     share = chunks // parts
     steps = model // OUT_COLS
     block = chunks // rings
@@ -113,7 +115,7 @@
     def incoming(k):
         g = part * share + k
         return remote(
-            enc.at[:, cols(g, IN_COLS)], held.at[g], in_send.at[k], in_recv.at[k], across
+            enc.at[:, cols(g, in_cols)], held.at[g], in_send.at[k], in_recv.at[k], across
         )
 
     def forward(k, j):
@@ -185,13 +187,13 @@
     load.wait()
 
     def relay(g):
-        here = cols(g, IN_COLS)
+        here = cols(g, in_cols)
         both = raw[here]
         flat[here, :width] = both[:, 0, :]
         flat[here, width:] = both[:, 1, :]
 
     def project(g):
-        acc[...] += dot(held[g], flat[cols(g, IN_COLS), :])
+        acc[...] += dot(held[g], flat[cols(g, in_cols), :])
 
     def relay_all(g, carry):
         relay(g)
@@ -291,7 +293,7 @@
             total[old] = summed.astype(jnp.bfloat16)
             outgoing(old).start()
 
-        at = n - LAG
+        at = n - shift
 
         @pl.when(jnp.logical_and(at >= 0, at < pairs))
         def _():
@@ -316,7 +318,8 @@
 
         return carry
 
-    lax.fori_loop(0, max(steps, pairs + PAIR_LAG) + LAG, back, 0)
+    shift = jnp.where(odd, LAG, steps // WAIT) if staggered else LAG
+    lax.fori_loop(0, jnp.maximum(steps + LAG, pairs + PAIR_LAG + shift), back, 0)
 
     context = jnp.zeros((tokens, width), jnp.float32)
     for h in range(heads):
@@ -327,7 +330,7 @@
     ctx_copy.start()
 
     def weight_copy(q):
-        here = cols(q, IN_COLS)
+        here = cols(q, in_cols)
         return pltpu.make_async_copy(final_weight.at[here], weight_out.at[here], weight_sem.at[q])
 
     def finish(q, carry):
@@ -336,7 +339,7 @@
             crossing(j * block + q, {"dp": far[j]}).wait_recv()
             summed = summed + x_in[j * block + q].astype(jnp.float32)
         mean = (summed * (1.0 / rings)).astype(jnp.bfloat16)
-        final_weight[cols(q, IN_COLS)] = mean.reshape(IN_COLS, 2, width)
+        final_weight[cols(q, in_cols)] = mean.reshape(in_cols, 2, width)
         weight_copy(q).start()
         return carry
 
@@ -389,7 +392,8 @@
     keys, model = enc_states.shape[2:]
     tokens, width = queries.shape[2:]
     heads = width // HEAD
-    chunks = model // IN_COLS
+    in_cols = min(IN_COLS, model // rings)
+    chunks = model // in_cols
     share, steps, block, pairs = (
         chunks // parts, model // OUT_COLS, chunks // rings, chunks // 2,
     )
@@ -409,7 +413,7 @@
         in_specs=[hbm, vmem, vmem, vmem, hbm, vmem],
         out_specs=(hbm, hbm, hbm),
         scratch_shapes=[
-            pltpu.VMEM((chunks, keys, IN_COLS), b16),
+            pltpu.VMEM((chunks, keys, in_cols), b16),
             pltpu.VMEM((model, 2, width), b16),
             pltpu.VMEM((model, 2 * width), b16),
             pltpu.VMEM((keys, 2 * width), f32),
@@ -421,11 +425,11 @@
             pltpu.VMEM((steps, keys, OUT_COLS), b16),
             pltpu.VMEM((parts, steps, rows, OUT_COLS), b16),
             pltpu.VMEM((steps, rows, OUT_COLS), b16),
-            pltpu.VMEM((chunks, IN_COLS, 2 * width), b16),
-            pltpu.VMEM((pairs, IN_COLS, 2 * width), b16),
-            pltpu.VMEM((block, IN_COLS, 2 * width), f32),
-            pltpu.VMEM((crossed, IN_COLS, 2 * width), b16),
-            pltpu.VMEM((crossed, IN_COLS, 2 * width), b16),
+            pltpu.VMEM((chunks, in_cols, 2 * width), b16),
+            pltpu.VMEM((pairs, in_cols, 2 * width), b16),
+            pltpu.VMEM((block, in_cols, 2 * width), f32),
+            pltpu.VMEM((crossed, in_cols, 2 * width), b16),
+            pltpu.VMEM((crossed, in_cols, 2 * width), b16),
             dma,
             dma((share,)),
             dma((share,)),

time: 104 us -> 104 us (level)
  no operation moved by 1% of the time
where the time goes in v3:
time: 104 us
  Pallas kernels  103 us (99%)
    pallas_call x1, Pallas kernels, body(): pl.pallas_call(functools.partial(kernel, phases, rings, parts), out_shape...  101 us
    pallas_call x1, Pallas kernels, body(): pl.pallas_call(hand_over, out_shape=tuple((jax.ShapeDtypeStruct(r.shape,...  2.48 us

profile of v3, /device:TPU:0, one launch (start us, length us, event | category | flops | bytes accessed | tf_op | source)
XLA Modules:
  0.0 103.6 jit_solution(480528546732648215)
XLA Ops:
  0.6 100.5 %shard_map.85 = (bf16[128,256]{1,0:T(8,128)(2,1)}, bf16[128,4096]{1,0:T(8,128)(2,1)}, bf16[1024,2,256]{2,1,0:T(2,128)(2,1)}) custom-call(bf16[256,4096]{1,0:T(8,128)(2,1)} %bitcast.10, bf16[128,256]{1,0:T(8,128)(2,1)} %bitcast.13, s32[1,128]{1,0:T(1,128)} %bitcast.17, s32[1,256]{1,0:T(1,128)} %bitcast.16, bf16[4096,2,256]{2,1,0:T(2,128)(2,1)} %bitcast.9, ...), custom_call_target="tpu_custom_call" | custom-call | flops 3221225472 | bytes 9437184 | tf_op jit(solution)/shard_map/pallas_call | solution.py:406
  101.2 2.5 %shard_map.86 = (bf16[128,256]{1,0:T(8,128)(2,1)}, bf16[128,4096]{1,0:T(8,128)(2,1)}, bf16[1024,2,256]{2,1,0:T(2,128)(2,1)}) custom-call(bf16[128,256]{1,0:T(8,128)(2,1)} %get-tuple-element.9.ctx, bf16[128,4096]{1,0:T(8,128)(2,1)} %get-tuple-element.10.state, bf16[1024,2,256]{2,1,0:T(2,128)(2,1)} %get-tuple-element.11.weight), custom_call_target="tpu_custom_call" | custom-call | tf_op jit(solution)/shard_map/pallas_call | solution.py:462
